TPU v7x, 256 devices: a whole 4x4x8 slice. The times are simulated.
256 devices in a mesh: gx: 64 (over z, x, core), gz: 4 (over y).
Axes of the slice: x: 4, y: 4, z: 8, core: 2. Of those that a mesh axis runs over, the one named last changes fastest.
Arguments:
- velocity: float32 [3, 4096, 32, 256], P(None, 'gx', 'gz'), may hold values from -6 to 6
Outputs:
- smoothed: float32 [9, 4096, 32, 256], P(None, 'gx', 'gz')
- vertical_derivative: float32 [9, 4096, 32, 256], P(None, 'gx', 'gz')
All inputs are finite; a program needn't handle non-finite values.
Results may differ from a plain program's by a relative error of at most 0.00014.
Values sent between devices are 32-bit elements; how exact they have to be, the bound alone decides.
A program may use at most 128 MiB of HBM per device.

v0:
```python
import math

import jax
import jax.numpy as jnp
import numpy as np
from jax import lax
from jax.sharding import PartitionSpec as P


def extended(shard, sides, width):
    for axis, dim in sides:
        devices, length = (lax.axis_size(axis), shard.shape[dim])
        up = [(i, (i + 1) % devices) for i in range(devices)]
        down = [(j, i) for i, j in up]
        last = lax.slice_in_dim(shard, length - width, length, axis=dim)
        initial = lax.slice_in_dim(shard, 0, width, axis=dim)
        before = lax.ppermute(last, axis, up)
        after = lax.ppermute(initial, axis, down)
        shard = jnp.concatenate([before, shard, after], axis=dim)
    return shard


def passed_along(block, axis, distance):
    devices = range(lax.axis_size(axis))
    route = [((i - distance) % len(devices), i) for i in devices]
    return lax.ppermute(block, axis, route)


def products(velocity):
    stream = velocity[0]
    span = velocity[1]
    upward = velocity[2]
    return jnp.stack(
        [
            stream,
            span,
            upward,
            stream * stream,
            stream * span,
            stream * upward,
            span * span,
            span * upward,
            upward * upward,
        ]
    )


def vertical_terms(padded, layers):

    def plane(offset):
        return padded[:, :, 3 + offset : 3 + offset + layers]

    return (
        45.0 * (plane(1) - plane(-1)) - 9.0 * (plane(2) - plane(-2)) + (plane(3) - plane(-3))
    ) / 60.0


def hyperbolic_sine(value):
    return 0.5 * (math.exp(value) - math.exp(-value))


def interior_inverse(inner, stiffness):
    half_ratio = 0.5 / math.sqrt(stiffness)
    angle = 2.0 * math.log(half_ratio + math.sqrt(half_ratio * half_ratio + 1.0))
    scale_term = stiffness * hyperbolic_sine(angle) * hyperbolic_sine((inner + 1) * angle)
    table_rows = []
    for row_index in range(inner):
        row_values = []
        for col_index in range(inner):
            lower_index = min(row_index, col_index)
            upper_index = max(row_index, col_index)
            row_values.append(
                hyperbolic_sine((lower_index + 1) * angle)
                * hyperbolic_sine((inner - upper_index) * angle)
                / scale_term
            )
        table_rows.append(row_values)
    return np.array(table_rows)


def shards(velocity):
    cells = velocity.shape[1]
    layers = velocity.shape[2]
    fields = products(velocity)
    padded = extended(fields, (("gz", 2),), 3)
    vertical = vertical_terms(padded, layers)
    members = lax.axis_size("gx")
    sections = members.bit_length() - 1
    stiffness = (cells * members / 8.0) ** 2
    inner = cells - 1
    inverse_table = interior_inverse(inner, stiffness)
    inverse = jnp.asarray(inverse_table.astype(np.float32))
    partial_sol = jnp.einsum(
        "ij,fjzy->fizy", inverse, fields[:, :inner], precision=lax.Precision.HIGHEST
    )
    following = passed_along(partial_sol[:, 0], "gx", -1)
    reduced = fields[:, inner] + stiffness * partial_sol[:, inner - 1] + stiffness * following
    off_coef = float(-stiffness * stiffness * inverse_table[0, inner - 1])
    diag_coef = float(1.0 + 2.0 * stiffness - 2.0 * stiffness * stiffness * inverse_table[0, 0])
    for section in range(sections):
        stride = 1 << section
        lower_rhs = passed_along(reduced, "gx", stride)
        upper_rhs = passed_along(reduced, "gx", -stride)
        weight_ratio = off_coef / diag_coef
        reduced = reduced - weight_ratio * (lower_rhs + upper_rhs)
        diag_coef = diag_coef - 2.0 * off_coef * weight_ratio
        off_coef = -off_coef * weight_ratio
    interface = reduced * (1.0 / (diag_coef + 2.0 * off_coef))
    preceding = passed_along(interface, "gx", 1)
    interior = (
        partial_sol
        + stiffness * preceding[:, None] * inverse[:, 0][None, :, None, None]
        + stiffness * interface[:, None] * inverse[:, inner - 1][None, :, None, None]
    )
    smoothed = jnp.concatenate([interior, interface[:, None]], axis=1)
    return (smoothed, vertical)


def solution(mesh):
    placed = (P(None, "gx", "gz", None),)
    return jax.shard_map(
        shards,
        mesh=mesh,
        in_specs=placed,
        out_specs=(P(None, "gx", "gz", None), P(None, "gx", "gz", None)),
        check_vma=False,
    )
```

profile of v0, /device:TPU:30, one launch (start us, length us, event | category | flops | bytes accessed | tf_op | source)
XLA Modules:
  0.0 95.8 jit_solution(13066196558457581122)
XLA Ops:
  0.6 2.0 %fusion.15 = (f32[3,64,8,256]{3,1,2,0:T(8,128)S(1)}, f32[9,64,8,256]{3,1,2,0:T(8,128)S(1)}) fusion(f32[3,64,8,256]{3,2,1,0:T(8,128)} %param.2), kind=kLoop, calls=%fused_computation.48 | loop fusion | bytes 4718592 | tf_op args[0]
  2.6 0.0 copy-start
  2.7 0.1 multiply_dynamic-update-slice_fusion.4
  2.8 0.1 multiply_dynamic-update-slice_fusion.3
  2.9 0.1 multiply_dynamic-update-slice_fusion.1
  3.0 0.4 copy-done
  3.4 4.5 %fusion.12 = f32[9,8,256,63]{2,3,1,0:T(8,128)S(1)} fusion(f32[63,63,1,1]{1,0,3,2:T(8,128)S(1)} %copy-done, f32[9,64,8,256]{3,1,2,0:T(8,128)S(1)} %multiply_dynamic-update-slice_fusion), kind=kOutput, calls=%fused_computation.22 | convolution fusion | flops 877879296 | bytes 9379332 | tf_op jit(solution)/shard_map/ij,fjzy->fizy/dot_general | solution.py:93
  7.8 2.7 %copy.21 = f32[9,8,256,63]{2,1,0,3:T(8,128)S(1)} copy(f32[9,8,256,63]{2,3,1,0:T(8,128)S(1)} %fusion.12) | data formatting | bytes 9289728 | tf_op jit(solution)/shard_map/ij,fjzy->fizy/dot_general | solution.py:93
  10.6 0.3 collective-permute-start
  10.9 0.0 copy-start.1
  10.9 0.0 copy-start.2
  10.9 0.1 slice_add_fusion
  11.0 1.9 %collective-permute-done = f32[9,8,256]{2,1,0:T(8,128)S(1)} collective-permute-done((f32[9,8,256]{2,1,0:T(8,128)S(1)}, f32[9,8,256]{2,1,0:T(8,128)S(1)}, u32[]{:S(2)}, u32[]{:S(2)}) %collective-permute-start) | collective-permute-done | bytes 73760 | tf_op jit(solution)/shard_map/ppermute | solution.py:26
  12.9 3.4 %collective-permute-start.1 = (f32[9,8,256]{2,1,0:T(8,128)S(1)}, f32[9,8,256]{2,1,0:T(8,128)S(1)}, u32[]{:S(2)}, u32[]{:S(2)}) collective-permute-start(f32[9,8,256]{2,1,0:T(8,128)S(1)} %bitcast_add_fusion), channel_id=1, source_target_pairs={{252,0},{0,4},{4,8},{8,12},{12,16},{16,20},{20,24},{24,28},{28,32}... | collective-permute-start | bytes 221192 | tf_op jit(solution)/shard_map/ppermute | solution.py:26
  16.3 0.0 collective-permute-start.2
  16.3 0.9 collective-permute-done.1
  17.2 1.1 %collective-permute-done.2 = f32[9,8,256]{2,1,0:T(8,128)S(1)} collective-permute-done((f32[9,8,256]{2,1,0:T(8,128)S(1)}, f32[9,8,256]{2,1,0:T(8,128)S(1)}, u32[]{:S(2)}, u32[]{:S(2)}) %collective-permute-start.2) | collective-permute-done | bytes 73760 | tf_op jit(solution)/shard_map/ppermute | solution.py:26
  18.3 3.9 %collective-permute-start.3 = (f32[9,8,256]{2,1,0:T(8,128)S(1)}, f32[9,8,256]{2,1,0:T(8,128)S(1)}, u32[]{:S(2)}, u32[]{:S(2)}) collective-permute-start(f32[9,8,256]{2,1,0:T(8,128)S(1)} %multiply_subtract_fusion.5), channel_id=1, source_target_pairs={{248,0},{252,4},{0,8},{4,12},{8,16},{12,20},{16,24},{20,28},{24,32... | collective-permute-start | bytes 221192 | tf_op jit(solution)/shard_map/ppermute | solution.py:26
  22.2 0.0 collective-permute-start.4
  22.2 2.1 %collective-permute-done.3 = f32[9,8,256]{2,1,0:T(8,128)S(1)} collective-permute-done((f32[9,8,256]{2,1,0:T(8,128)S(1)}, f32[9,8,256]{2,1,0:T(8,128)S(1)}, u32[]{:S(2)}, u32[]{:S(2)}) %collective-permute-start.3) | collective-permute-done | bytes 73760 | tf_op jit(solution)/shard_map/ppermute | solution.py:26
  24.4 4.6 %collective-permute-done.4 = f32[9,8,256]{2,1,0:T(8,128)S(1)} collective-permute-done((f32[9,8,256]{2,1,0:T(8,128)S(1)}, f32[9,8,256]{2,1,0:T(8,128)S(1)}, u32[]{:S(2)}, u32[]{:S(2)}) %collective-permute-start.4) | collective-permute-done | bytes 73760 | tf_op jit(solution)/shard_map/ppermute | solution.py:26
  29.0 0.1 collective-permute-start.5
  29.1 3.5 %collective-permute-start.6 = (f32[9,8,256]{2,1,0:T(8,128)S(1)}, f32[9,8,256]{2,1,0:T(8,128)S(1)}, u32[]{:S(2)}, u32[]{:S(2)}) collective-permute-start(f32[9,8,256]{2,1,0:T(8,128)S(1)} %multiply_subtract_fusion.4), channel_id=1, source_target_pairs={{16,0},{20,4},{24,8},{28,12},{32,16},{36,20},{40,24},{44,28},{48,3... | collective-permute-start | bytes 221192 | tf_op jit(solution)/shard_map/ppermute | solution.py:26
  32.6 3.9 %collective-permute-done.5 = f32[9,8,256]{2,1,0:T(8,128)S(1)} collective-permute-done((f32[9,8,256]{2,1,0:T(8,128)S(1)}, f32[9,8,256]{2,1,0:T(8,128)S(1)}, u32[]{:S(2)}, u32[]{:S(2)}) %collective-permute-start.5) | collective-permute-done | bytes 73760 | tf_op jit(solution)/shard_map/ppermute | solution.py:26
  36.5 0.0 collective-permute-done.6
  36.5 2.0 %collective-permute-start.7 = (f32[9,8,256]{2,1,0:T(8,128)S(1)}, f32[9,8,256]{2,1,0:T(8,128)S(1)}, u32[]{:S(2)}, u32[]{:S(2)}) collective-permute-start(f32[9,8,256]{2,1,0:T(8,128)S(1)} %multiply_subtract_fusion.3), channel_id=1, source_target_pairs={{224,0},{228,4},{232,8},{236,12},{240,16},{244,20},{248,24},{252,2... | collective-permute-start | bytes 221192 | tf_op jit(solution)/shard_map/ppermute | solution.py:26
  38.5 8.4 %collective-permute-start.8 = (f32[9,8,256]{2,1,0:T(8,128)S(1)}, f32[9,8,256]{2,1,0:T(8,128)S(1)}, u32[]{:S(2)}, u32[]{:S(2)}) collective-permute-start(f32[9,8,256]{2,1,0:T(8,128)S(1)} %multiply_subtract_fusion.3), channel_id=1, source_target_pairs={{32,0},{36,4},{40,8},{44,12},{48,16},{52,20},{56,24},{60,28},{64,3... | collective-permute-start | bytes 221192 | tf_op jit(solution)/shard_map/ppermute | solution.py:26
  46.9 0.2 fusion.14
  47.2 0.3 collective-permute-start.14
  47.5 1.8 %collective-permute-start.13 = (f32[9,64,3,256]{3,1,2,0:T(8,128)S(1)}, f32[9,64,3,256]{3,1,2,0:T(8,128)S(1)}, u32[]{:S(2)}, u32[]{:S(2)}) collective-permute-start(f32[9,64,3,256]{3,1,2,0:T(8,128)S(1)} %get-tuple-element.4), channel_id=1, source_target_pairs={{1,0},{2,1},{3,2},{0,3},{5,4},{6,5},{7,6},{4,7},{9,8},{10,9},{11,1... | collective-permute-start | bytes 5308424 | tf_op jit(solution)/shard_map/ppermute | solution.py:18
  49.3 0.0 collective-permute-done.7
  49.3 0.0 collective-permute-done.8
  49.3 1.2 %collective-permute-start.9 = (f32[9,8,256]{2,1,0:T(8,128)S(1)}, f32[9,8,256]{2,1,0:T(8,128)S(1)}, u32[]{:S(2)}, u32[]{:S(2)}) collective-permute-start(f32[9,8,256]{2,1,0:T(8,128)S(1)} %multiply_subtract_fusion.2), channel_id=1, source_target_pairs={{192,0},{196,4},{200,8},{204,12},{208,16},{212,20},{216,24},{220,2... | collective-permute-start | bytes 221192 | tf_op jit(solution)/shard_map/ppermute | solution.py:26
  50.5 3.0 %collective-permute-start.10 = (f32[9,8,256]{2,1,0:T(8,128)S(1)}, f32[9,8,256]{2,1,0:T(8,128)S(1)}, u32[]{:S(2)}, u32[]{:S(2)}) collective-permute-start(f32[9,8,256]{2,1,0:T(8,128)S(1)} %multiply_subtract_fusion.2), channel_id=1, source_target_pairs={{64,0},{68,4},{72,8},{76,12},{80,16},{84,20},{88,24},{92,28},{96,3... | collective-permute-start | bytes 221192 | tf_op jit(solution)/shard_map/ppermute | solution.py:26
  53.5 2.3 %collective-permute-done.9 = f32[9,8,256]{2,1,0:T(8,128)S(1)} collective-permute-done((f32[9,8,256]{2,1,0:T(8,128)S(1)}, f32[9,8,256]{2,1,0:T(8,128)S(1)}, u32[]{:S(2)}, u32[]{:S(2)}) %collective-permute-start.9) | collective-permute-done | bytes 73760 | tf_op jit(solution)/shard_map/ppermute | solution.py:26
  55.8 0.4 collective-permute-done.10
  56.2 4.4 %collective-permute-start.11 = (f32[9,8,256]{2,1,0:T(8,128)S(1)}, f32[9,8,256]{2,1,0:T(8,128)S(1)}, u32[]{:S(2)}, u32[]{:S(2)}) collective-permute-start(f32[9,8,256]{2,1,0:T(8,128)S(1)} %multiply_subtract_fusion.1), channel_id=1, source_target_pairs={{128,0},{132,4},{136,8},{140,12},{144,16},{148,20},{152,24},{156,2... | collective-permute-start | bytes 221192 | tf_op jit(solution)/shard_map/ppermute | solution.py:26
  60.6 4.4 %collective-permute-done.11 = f32[9,8,256]{2,1,0:T(8,128)S(1)} collective-permute-done((f32[9,8,256]{2,1,0:T(8,128)S(1)}, f32[9,8,256]{2,1,0:T(8,128)S(1)}, u32[]{:S(2)}, u32[]{:S(2)}) %collective-permute-start.11) | collective-permute-done | bytes 73760 | tf_op jit(solution)/shard_map/ppermute | solution.py:26
  65.0 0.3 collective-permute-start.12
  65.3 3.8 %collective-permute-done.12 = f32[9,8,256]{2,1,0:T(8,128)S(1)} collective-permute-done((f32[9,8,256]{2,1,0:T(8,128)S(1)}, f32[9,8,256]{2,1,0:T(8,128)S(1)}, u32[]{:S(2)}, u32[]{:S(2)}) %collective-permute-start.12) | collective-permute-done | bytes 73760 | tf_op jit(solution)/shard_map/ppermute | solution.py:26
  69.1 0.0 copy-done.1
  69.1 0.0 copy-done.2
  69.1 3.0 %multiply_add_fusion = f32[9,63,8,256]{3,2,0,1:T(8,128)S(1)} fusion(f32[63]{0:T(128)S(1)} %copy-done.1, f32[9,8,256]{2,1,0:T(8,128)S(1)} %get-tuple-element.10, f32[63]{0:T(128)S(1)} %copy-done.2, f32[9,8,256]{2,1,0:T(8,128)S(1)} %broadcast_multiply_fusion.2, f32[9,8,256,63]{2,3,1,0:T(8,128)S(1)} %fusion.12), kind=kLoop, calls=%fused_computation.26 | loop fusion | flops 4644864 | bytes 9437688 | tf_op jit(solution)/shard_map/add | solution.py:111
  72.1 0.3 pad_maximum_fusion.2
  72.4 2.7 %copy.10 = f32[9,64,8,256]{3,2,1,0:T(8,128)} copy(f32[9,64,8,256]{3,2,0,1:T(8,128)S(1)} %pad_maximum_fusion.2) | data formatting | bytes 9437184
  75.1 10.9 %collective-permute-done.14 = f32[9,64,3,256]{3,1,2,0:T(8,128)S(1)} collective-permute-done((f32[9,64,3,256]{3,1,2,0:T(8,128)S(1)}, f32[9,64,3,256]{3,1,2,0:T(8,128)S(1)}, u32[]{:S(2)}, u32[]{:S(2)}) %collective-permute-start.14) | collective-permute-done | bytes 1769504 | tf_op jit(solution)/shard_map/ppermute | solution.py:17
  86.0 1.3 %collective-permute-done.13 = f32[9,64,3,256]{3,1,2,0:T(8,128)S(1)} collective-permute-done((f32[9,64,3,256]{3,1,2,0:T(8,128)S(1)}, f32[9,64,3,256]{3,1,2,0:T(8,128)S(1)}, u32[]{:S(2)}, u32[]{:S(2)}) %collective-permute-start.13) | collective-permute-done | bytes 1769504 | tf_op jit(solution)/shard_map/ppermute | solution.py:18
  87.3 3.6 %fusion.5 = f32[9,64,8,256]{3,1,2,0:T(8,128)S(1)} fusion(f32[9,64,8,256]{3,1,2,0:T(8,128)S(1)} %multiply_dynamic-update-slice_fusion, f32[9,64,3,256]{3,1,2,0:T(8,128)S(1)} %collective-permute-done.14, f32[9,64,3,256]{3,1,2,0:T(8,128)S(1)} %collective-permute-done.13), kind=kLoop, calls=%fused_computation.13 | loop fusion | flops 16515072 | bytes 12976128 | tf_op jit(solution)/shard_map/div | solution.py:53
  90.9 4.9 %copy.11 = f32[9,64,8,256]{3,2,1,0:T(8,128)} copy(f32[9,64,8,256]{3,1,2,0:T(8,128)S(1)} %fusion.5) | data formatting | bytes 9437184
  (12 shorter events, 0.3 us)
Async XLA Ops:
  2.6 0.8 copy-start
  10.6 2.3 %collective-permute-start = (f32[9,8,256]{2,1,0:T(8,128)S(1)}, f32[9,8,256]{2,1,0:T(8,128)S(1)}, u32[]{:S(2)}, u32[]{:S(2)}) collective-permute-start(f32[9,8,256]{2,1,0:T(8,128)S(1)} %get-tuple-element.6), channel_id=1, source_target_pairs={{4,0},{8,4},{12,8},{16,12},{20,16},{24,20},{28,24},{32,28},{36,32}... | collective-permute-start | bytes 221192 | tf_op jit(solution)/shard_map/ppermute | solution.py:26
  10.9 58.1 %copy-start.1 = (f32[63]{0:T(128)S(1)}, f32[63]{0:T(128)}, u32[]{:S(2)}) copy-start(f32[63]{0:T(128)} %constant.32) | copy-start | bytes 760
  10.9 58.1 %copy-start.2 = (f32[63]{0:T(128)S(1)}, f32[63]{0:T(128)}, u32[]{:S(2)}) copy-start(f32[63]{0:T(128)} %constant.30) | copy-start | bytes 760
  12.9 4.3 %collective-permute-start.1 = (f32[9,8,256]{2,1,0:T(8,128)S(1)}, f32[9,8,256]{2,1,0:T(8,128)S(1)}, u32[]{:S(2)}, u32[]{:S(2)}) collective-permute-start(f32[9,8,256]{2,1,0:T(8,128)S(1)} %bitcast_add_fusion), channel_id=1, source_target_pairs={{252,0},{0,4},{4,8},{8,12},{12,16},{16,20},{20,24},{24,28},{28,32}... | collective-permute-start | bytes 221192 | tf_op jit(solution)/shard_map/ppermute | solution.py:26
  16.3 2.0 %collective-permute-start.2 = (f32[9,8,256]{2,1,0:T(8,128)S(1)}, f32[9,8,256]{2,1,0:T(8,128)S(1)}, u32[]{:S(2)}, u32[]{:S(2)}) collective-permute-start(f32[9,8,256]{2,1,0:T(8,128)S(1)} %bitcast_add_fusion), channel_id=1, source_target_pairs={{4,0},{8,4},{12,8},{16,12},{20,16},{24,20},{28,24},{32,28},{36,32}... | collective-permute-start | bytes 221192 | tf_op jit(solution)/shard_map/ppermute | solution.py:26
  18.3 6.0 %collective-permute-start.3 = (f32[9,8,256]{2,1,0:T(8,128)S(1)}, f32[9,8,256]{2,1,0:T(8,128)S(1)}, u32[]{:S(2)}, u32[]{:S(2)}) collective-permute-start(f32[9,8,256]{2,1,0:T(8,128)S(1)} %multiply_subtract_fusion.5), channel_id=1, source_target_pairs={{248,0},{252,4},{0,8},{4,12},{8,16},{12,20},{16,24},{20,28},{24,32... | collective-permute-start | bytes 221192 | tf_op jit(solution)/shard_map/ppermute | solution.py:26
  22.2 6.7 %collective-permute-start.4 = (f32[9,8,256]{2,1,0:T(8,128)S(1)}, f32[9,8,256]{2,1,0:T(8,128)S(1)}, u32[]{:S(2)}, u32[]{:S(2)}) collective-permute-start(f32[9,8,256]{2,1,0:T(8,128)S(1)} %multiply_subtract_fusion.5), channel_id=1, source_target_pairs={{8,0},{12,4},{16,8},{20,12},{24,16},{28,20},{32,24},{36,28},{40,32... | collective-permute-start | bytes 221192 | tf_op jit(solution)/shard_map/ppermute | solution.py:26
  29.0 7.5 %collective-permute-start.5 = (f32[9,8,256]{2,1,0:T(8,128)S(1)}, f32[9,8,256]{2,1,0:T(8,128)S(1)}, u32[]{:S(2)}, u32[]{:S(2)}) collective-permute-start(f32[9,8,256]{2,1,0:T(8,128)S(1)} %multiply_subtract_fusion.4), channel_id=1, source_target_pairs={{240,0},{244,4},{248,8},{252,12},{0,16},{4,20},{8,24},{12,28},{16,... | collective-permute-start | bytes 221192 | tf_op jit(solution)/shard_map/ppermute | solution.py:26
  29.1 7.4 %collective-permute-start.6 = (f32[9,8,256]{2,1,0:T(8,128)S(1)}, f32[9,8,256]{2,1,0:T(8,128)S(1)}, u32[]{:S(2)}, u32[]{:S(2)}) collective-permute-start(f32[9,8,256]{2,1,0:T(8,128)S(1)} %multiply_subtract_fusion.4), channel_id=1, source_target_pairs={{16,0},{20,4},{24,8},{28,12},{32,16},{36,20},{40,24},{44,28},{48,3... | collective-permute-start | bytes 221192 | tf_op jit(solution)/shard_map/ppermute | solution.py:26
  36.5 12.8 %collective-permute-start.7 = (f32[9,8,256]{2,1,0:T(8,128)S(1)}, f32[9,8,256]{2,1,0:T(8,128)S(1)}, u32[]{:S(2)}, u32[]{:S(2)}) collective-permute-start(f32[9,8,256]{2,1,0:T(8,128)S(1)} %multiply_subtract_fusion.3), channel_id=1, source_target_pairs={{224,0},{228,4},{232,8},{236,12},{240,16},{244,20},{248,24},{252,2... | collective-permute-start | bytes 221192 | tf_op jit(solution)/shard_map/ppermute | solution.py:26
  38.5 10.8 %collective-permute-start.8 = (f32[9,8,256]{2,1,0:T(8,128)S(1)}, f32[9,8,256]{2,1,0:T(8,128)S(1)}, u32[]{:S(2)}, u32[]{:S(2)}) collective-permute-start(f32[9,8,256]{2,1,0:T(8,128)S(1)} %multiply_subtract_fusion.3), channel_id=1, source_target_pairs={{32,0},{36,4},{40,8},{44,12},{48,16},{52,20},{56,24},{60,28},{64,3... | collective-permute-start | bytes 221192 | tf_op jit(solution)/shard_map/ppermute | solution.py:26
  47.2 38.8 %collective-permute-start.14 = (f32[9,64,3,256]{3,1,2,0:T(8,128)S(1)}, f32[9,64,3,256]{3,1,2,0:T(8,128)S(1)}, u32[]{:S(2)}, u32[]{:S(2)}) collective-permute-start(f32[9,64,3,256]{3,1,2,0:T(8,128)S(1)} %get-tuple-element.5), channel_id=1, source_target_pairs={{0,1},{1,2},{2,3},{3,0},{4,5},{5,6},{6,7},{7,4},{8,9},{9,10},{10,1... | collective-permute-start | bytes 5308424 | tf_op jit(solution)/shard_map/ppermute | solution.py:17
  47.5 39.8 %collective-permute-start.13 = (f32[9,64,3,256]{3,1,2,0:T(8,128)S(1)}, f32[9,64,3,256]{3,1,2,0:T(8,128)S(1)}, u32[]{:S(2)}, u32[]{:S(2)}) collective-permute-start(f32[9,64,3,256]{3,1,2,0:T(8,128)S(1)} %get-tuple-element.4), channel_id=1, source_target_pairs={{1,0},{2,1},{3,2},{0,3},{5,4},{6,5},{7,6},{4,7},{9,8},{10,9},{11,1... | collective-permute-start | bytes 5308424 | tf_op jit(solution)/shard_map/ppermute | solution.py:18
  49.3 6.5 %collective-permute-start.9 = (f32[9,8,256]{2,1,0:T(8,128)S(1)}, f32[9,8,256]{2,1,0:T(8,128)S(1)}, u32[]{:S(2)}, u32[]{:S(2)}) collective-permute-start(f32[9,8,256]{2,1,0:T(8,128)S(1)} %multiply_subtract_fusion.2), channel_id=1, source_target_pairs={{192,0},{196,4},{200,8},{204,12},{208,16},{212,20},{216,24},{220,2... | collective-permute-start | bytes 221192 | tf_op jit(solution)/shard_map/ppermute | solution.py:26
  50.5 5.7 %collective-permute-start.10 = (f32[9,8,256]{2,1,0:T(8,128)S(1)}, f32[9,8,256]{2,1,0:T(8,128)S(1)}, u32[]{:S(2)}, u32[]{:S(2)}) collective-permute-start(f32[9,8,256]{2,1,0:T(8,128)S(1)} %multiply_subtract_fusion.2), channel_id=1, source_target_pairs={{64,0},{68,4},{72,8},{76,12},{80,16},{84,20},{88,24},{92,28},{96,3... | collective-permute-start | bytes 221192 | tf_op jit(solution)/shard_map/ppermute | solution.py:26
  56.2 8.7 %collective-permute-start.11 = (f32[9,8,256]{2,1,0:T(8,128)S(1)}, f32[9,8,256]{2,1,0:T(8,128)S(1)}, u32[]{:S(2)}, u32[]{:S(2)}) collective-permute-start(f32[9,8,256]{2,1,0:T(8,128)S(1)} %multiply_subtract_fusion.1), channel_id=1, source_target_pairs={{128,0},{132,4},{136,8},{140,12},{144,16},{148,20},{152,24},{156,2... | collective-permute-start | bytes 221192 | tf_op jit(solution)/shard_map/ppermute | solution.py:26
  65.0 4.1 %collective-permute-start.12 = (f32[9,8,256]{2,1,0:T(8,128)S(1)}, f32[9,8,256]{2,1,0:T(8,128)S(1)}, u32[]{:S(2)}, u32[]{:S(2)}) collective-permute-start(f32[9,8,256]{2,1,0:T(8,128)S(1)} %get-tuple-element.11), channel_id=1, source_target_pairs={{252,0},{0,4},{4,8},{8,12},{12,16},{16,20},{20,24},{24,28},{28,32}... | collective-permute-start | bytes 221192 | tf_op jit(solution)/shard_map/ppermute | solution.py:26
where the time goes:
time: 96 us; the launch traced here: 95.8 us
  waiting for transfers between devices  37.5 us (39%)
  starting transfers between devices  32.7 us (34%)
  local copies, waits for them, and re-layouts  12.8 us (13%)
  other arithmetic  7.52 us (8%)
  matrix products  4.45 us (5%)
    ppermute x13, starting transfers between devices, passed_along(): return lax.ppermute(block, axis, route)  30.6 us
    ppermute x13, waiting for transfers between devices, passed_along(): return lax.ppermute(block, axis, route)  25.3 us
    ppermute x1, waiting for transfers between devices, extended(): before = lax.ppermute(last, axis, up)  10.9 us
    unnamed x9, local copies, waits for them, and re-layouts  9.92 us
    dot_general x1, matrix products, shards(): jnp.einsum('ij,fjzy->fizy', inverse, fields[:, :inner], precision=lax.Pre...  4.45 us
    div x1, other arithmetic, vertical_terms(): (45.0 * (plane(1) - plane(-1)) - 9.0 * (plane(2) - plane(-2)) + (plane(3)...  3.61 us
    add x1, other arithmetic, shards(): partial_sol + stiffness * preceding[:, None] * inverse[:, 0][None, :, Non...  3 us
    dot_general x1, local copies, waits for them, and re-layouts, shards(): jnp.einsum('ij,fjzy->fizy', inverse, fields[:, :inner], precision=lax.Pre...  2.69 us
  transfers between devices with their start and end apart: 15, of which 12 were waited for; matrix products, arithmetic and copies ran while one was open for 7% of the time, Pallas kernels for 0%

commit v1 on v0

v1 whole, which is shorter than its diff:
```python
import functools
import math

import jax
import jax.numpy as jnp
from jax import lax
from jax.experimental import pallas as pl
from jax.experimental.pallas import tpu as pltpu
from jax.sharding import PartitionSpec as P

MESH = pl.DeviceIdType.MESH
F32 = jnp.float32
GROUP = 8
CHUNKS = 8
HALO = 3
DERIV = (45.0 / 60.0, -9.0 / 60.0, 1.0 / 60.0)


def decay_of(stiffness):
    half = 0.5 / math.sqrt(stiffness)
    return math.exp(-2.0 * math.asinh(half)), 1.0 / math.sqrt(1.0 + 4.0 * stiffness)


def fields_of(a, b):
    return (
        a[0],
        a[1],
        a[2],
        a[0] * b[0],
        a[0] * b[1],
        a[0] * b[2],
        a[1] * b[1],
        a[1] * b[2],
        a[2] * b[2],
    )


def by_row(index, values):
    out = jnp.full(index.shape, values[0], F32)
    for i, value in enumerate(values[1:], 1):
        out = jnp.where(index == i, F32(value), out)
    return out


def vertical(center, halo, rows):
    total = None
    for k, coef in enumerate(DERIV, 1):
        upper = [
            pltpu.roll(jnp.where(rows >= k, c, h), 8 - k, 0) for c, h in zip(center, halo)
        ]
        lower = [
            pltpu.roll(jnp.where(rows < 8 - k, c, h), k, 0) for c, h in zip(center, halo)
        ]
        above = fields_of([F32(coef) * a for a in upper], upper)
        below = fields_of([F32(coef) * b for b in lower], lower)
        term = [a - b for a, b in zip(above, below)]
        total = term if total is None else [t + s for t, s in zip(total, term)]
    return total


def exchange_kernel(
    decay,
    scale,
    cells,
    blocks,
    v_hbm,
    local_ref,
    deriv_ref,
    carry_ref,
    v_ref,
    halo_ref,
    sums_ref,
    group_ref,
    total_ref,
    ring_ref,
    scan_ref,
    back_ref,
    load_sem,
    halo_send,
    halo_recv,
    send_sem,
    recv_sem,
):
    me = lax.axis_index("gx")
    y = lax.axis_index("gz")
    y_parts = lax.axis_size("gz")
    ring = blocks // GROUP
    z = me // GROUP
    p = lax.rem(me, GROUP)
    above_id = lax.rem(y + 1, y_parts)
    below_id = lax.rem(y + y_parts - 1, y_parts)
    wide = cells // CHUNKS
    rho = decay**cells
    jump = rho**GROUP

    barrier = pltpu.get_barrier_semaphore()
    for other in (above_id, below_id):
        pl.semaphore_signal(barrier, inc=1, device_id={"gz": other}, device_id_type=MESH)
    for k in range(1, GROUP):
        peer = z * GROUP + lax.rem(p + k, GROUP)
        pl.semaphore_signal(barrier, inc=1, device_id={"gx": peer}, device_id_type=MESH)
    for k in range(1, ring):
        peer = lax.rem(z + k, ring) * GROUP + p
        pl.semaphore_signal(barrier, inc=1, device_id={"gx": peer}, device_id_type=MESH)

    loads = []
    for n in range(CHUNKS):
        part = pl.ds(n * wide, wide)
        loads.append(
            pltpu.make_async_copy(v_hbm.at[:, part], v_ref.at[:, part], load_sem.at[n])
        )
    for load in loads:
        load.start()
    pl.semaphore_wait(barrier, 2 + (GROUP - 1) + (ring - 1))

    halos = []
    for n in range(CHUNKS):
        part = pl.ds(n * wide, wide)
        for side, (first, target) in enumerate(((0, below_id), (8 - HALO, above_id))):
            layers = pl.ds(first, HALO)
            halos.append(
                pltpu.make_async_remote_copy(
                    src_ref=v_hbm.at[:, part, layers],
                    dst_ref=halo_ref.at[:, part, layers],
                    send_sem=halo_send.at[n, side],
                    recv_sem=halo_recv.at[n, side],
                    device_id={"gz": target},
                    device_id_type=MESH,
                )
            )
    for halo in halos:
        halo.start()

    shape = v_ref.shape[2:]
    rows = lax.broadcasted_iota(jnp.int32, shape, 0)
    zero = jnp.zeros(shape, F32)

    def velocity(x):
        return [v_ref[c, x] for c in range(3)]

    def scaled_fields(x):
        v = velocity(x)
        return fields_of([F32(scale) * a for a in v], v)

    def forward(x, state):
        ahead, back, weight = state
        f = scaled_fields(x)
        ahead = tuple(F32(decay) * a + b for a, b in zip(ahead, f))
        back = tuple(a + weight * b for a, b in zip(back, f))
        for i in range(9):
            local_ref[i, x] = ahead[i]
        return ahead, back, weight * F32(decay)

    state = ((zero,) * 9, (zero,) * 9, jnp.ones(shape, F32))
    for n in range(CHUNKS):
        loads[n].wait()

        def some(j, state, n=n):
            for u in range(2):
                state = forward(n * wide + 2 * j + u, state)
            return state

        state = lax.fori_loop(0, wide // 2, some, state)
    for i in range(9):
        sums_ref[i] = state[0][i]
        sums_ref[9 + i] = state[1][i]

    def exchange(stage, source, target, peer_of, source_row, target_row, count):
        copies = []
        for k in range(1, count):
            copies.append(
                pltpu.make_async_remote_copy(
                    src_ref=source.at[:, pl.ds(source_row(k), 1)],
                    dst_ref=target.at[:, pl.ds(target_row, 1)],
                    send_sem=send_sem.at[stage, k],
                    recv_sem=recv_sem.at[stage, k],
                    device_id={"gx": peer_of(k)},
                    device_id_type=MESH,
                )
            )
        for copy in copies:
            copy.start()
        return copies

    def in_group(k):
        return lax.rem(p + k, GROUP)

    def group_peer(k):
        return z * GROUP + in_group(k)

    def ring_peer(k):
        return lax.rem(z + k, ring) * GROUP + p

    first = exchange(0, sums_ref, group_ref, group_peer, in_group, p, GROUP)

    def backward(j, behind):
        x = cells - 1 - j
        for i in range(9):
            local_ref[i, x] = local_ref[i, x] + behind[i]
        f = scaled_fields(x)
        return tuple(F32(decay) * (a + b) for a, b in zip(behind, f))

    def some_back(j, behind):
        for u in range(2):
            behind = backward(2 * j + u, behind)
        return behind

    lax.fori_loop(0, cells // 2, some_back, (zero,) * 9)

    def derive(n):
        halos[2 * n].wait_recv()
        halos[2 * n + 1].wait_recv()

        def one(j, _):
            x = n * wide + j
            out = vertical(velocity(x), [halo_ref[c, x] for c in range(3)], rows)
            for i in range(9):
                deriv_ref[i, x] = out[i]
            return 0

        lax.fori_loop(0, wide, one, 0)

    for copy in first:
        copy.wait_recv()
    ahead_weight = by_row(rows, [rho ** (GROUP - 1 - b) for b in range(GROUP)])
    back_weight = by_row(rows, [rho**b for b in range(GROUP)])
    mine = rows == p
    for i in range(18):
        held = jnp.where(mine, sums_ref[i], group_ref[i])
        group_ref[i] = held
        part = held * (ahead_weight if i < 9 else back_weight)
        total_ref[i] = jnp.broadcast_to(jnp.sum(part, axis=0, keepdims=True), shape)

    second = exchange(1, total_ref, ring_ref, ring_peer, lambda k: z, z, ring)

    for n in range(0, 2):
        derive(n)

    for copy in second:
        copy.wait_recv()
    closed = 1.0 / (1.0 - jump**ring)
    powers = [closed * jump**e for e in range(ring)]
    ahead_weight = by_row(lax.rem(z - rows + 2 * ring - 1, ring), powers)
    back_weight = by_row(lax.rem(rows - z + 2 * ring - 1, ring), powers)
    own = rows == z
    for i in range(18):
        held = jnp.where(own, total_ref[i], ring_ref[i])
        part = held * (ahead_weight if i < 9 else back_weight)
        entering = jnp.broadcast_to(jnp.sum(part, axis=0, keepdims=True), shape)
        if i < 9:
            run = jnp.where(rows == 0, entering, pltpu.roll(group_ref[i], 1, 0))
            for s in (1, 2, 4):
                moved = jnp.where(rows >= s, pltpu.roll(run, s, 0), F32(0))
                run = run + F32(rho**s) * moved
        else:
            run = jnp.where(rows == 7, entering, pltpu.roll(group_ref[i], 7, 0))
            for s in (1, 2, 4):
                moved = jnp.where(rows < 8 - s, pltpu.roll(run, 8 - s, 0), F32(0))
                run = run + F32(rho**s) * moved
        scan_ref[i] = run

    third = exchange(2, scan_ref, back_ref, group_peer, in_group, p, GROUP)

    for n in range(2, 5):
        derive(n)

    for copy in third:
        copy.wait_recv()
    for i in range(18):
        carry_ref[i] = jnp.where(mine, scan_ref[i], back_ref[i])

    for n in range(5, CHUNKS):
        derive(n)
    for copy in halos + first + second + third:
        copy.wait_send()


def write_kernel(decay, cells, local_ref, deriv_ref, carry_ref, out_s, out_d, held, sem_s, sem_d):
    wide = cells // CHUNKS
    copies = []
    for n in range(CHUNKS):
        part = pl.ds(n * wide, wide)
        copies.append(
            pltpu.make_async_copy(deriv_ref.at[:, part], out_d.at[:, part], sem_d.at[n])
        )
    for copy in copies:
        copy.start()
    ahead = [carry_ref[i] for i in range(9)]
    back = [carry_ref[9 + i] for i in range(9)]
    for n in range(CHUNKS):
        part = pl.ds(n * wide, wide)
        for x in range(n * wide, (n + 1) * wide):
            for i in range(9):
                held[i, x] = local_ref[i, x] + (
                    F32(decay ** (x + 1)) * ahead[i] + F32(decay ** (cells - x)) * back[i]
                )
        copy = pltpu.make_async_copy(held.at[:, part], out_s.at[:, part], sem_s.at[n])
        copy.start()
        copies.append(copy)
    for copy in copies:
        copy.wait()


def shards(velocity):
    comps, cells, layers, span = velocity.shape
    blocks = lax.axis_size("gx")
    ring = blocks // GROUP
    decay, scale = decay_of((cells * blocks / 8.0) ** 2)
    big = (9, cells, layers, span)
    small = (18, layers, span)
    local, deriv, carry = pl.pallas_call(
        functools.partial(exchange_kernel, decay, scale, cells, blocks),
        out_shape=(
            pltpu.VMEM(big, F32),
            pltpu.VMEM(big, F32),
            pltpu.VMEM(small, F32),
        ),
        in_specs=[pl.BlockSpec(memory_space=pl.ANY)],
        out_specs=[pl.BlockSpec(memory_space=pltpu.VMEM)] * 3,
        scratch_shapes=[
            pltpu.VMEM((comps, cells, layers, span), F32),
            pltpu.VMEM((comps, cells, layers, span), F32),
        ]
        + [pltpu.VMEM(small, F32)] * 6
        + [
            pltpu.SemaphoreType.DMA((CHUNKS,)),
            pltpu.SemaphoreType.DMA((CHUNKS, 2)),
            pltpu.SemaphoreType.DMA((CHUNKS, 2)),
            pltpu.SemaphoreType.DMA((3, GROUP)),
            pltpu.SemaphoreType.DMA((3, GROUP)),
        ],
        compiler_params=pltpu.CompilerParams(
            collective_id=0, has_side_effects=True, vmem_limit_bytes=24 << 20
        ),
        name="exchange",
    )(velocity)
    return pl.pallas_call(
        functools.partial(write_kernel, decay, cells),
        out_shape=(jax.ShapeDtypeStruct(big, F32), jax.ShapeDtypeStruct(big, F32)),
        in_specs=[pl.BlockSpec(memory_space=pltpu.VMEM)] * 3,
        out_specs=[pl.BlockSpec(memory_space=pltpu.HBM)] * 2,
        scratch_shapes=[
            pltpu.VMEM(big, F32),
            pltpu.SemaphoreType.DMA((CHUNKS,)),
            pltpu.SemaphoreType.DMA((CHUNKS,)),
        ],
        compiler_params=pltpu.CompilerParams(vmem_limit_bytes=24 << 20),
        name="write",
    )(local, deriv, carry)


def solution(mesh):
    spec = P(None, "gx", "gz", None)
    return jax.shard_map(
        shards, mesh=mesh, in_specs=(spec,), out_specs=(spec, spec), check_vma=False
    )
```

time: 96 us -> 32.3 us (0.34)
  the two profiles are of different devices: /device:TPU:30 before, /device:TPU:1 now
where the time goes in v1:
time: 32.3 us; the launch traced here: 32.2 us
  Pallas kernels  30.2 us (93%)
  local copies, waits for them, and re-layouts  1.4 us (4%)
  between operations  0.65 us (2%)
    pallas_call x1, Pallas kernels, shards(): pl.pallas_call(functools.partial(exchange_kernel, decay, scale, cells, bl...  26.4 us
    pallas_call x1, Pallas kernels, shards(): pl.pallas_call(functools.partial(write_kernel, decay, cells), out_shape=(...  3.84 us
    unnamed x2, local copies, waits for them, and re-layouts  1.4 us

profile of v1, /device:TPU:1, one launch (start us, length us, event | category | flops | bytes accessed | tf_op | source)
XLA Modules:
  0.0 32.2 jit_solution(7462940105942858013)
XLA Ops:
  0.6 0.0 copy-start
  0.6 1.4 %copy-done = f32[3,64,8,256]{3,2,1,0:T(8,128)S(1)} copy-done((f32[3,64,8,256]{3,2,1,0:T(8,128)S(1)}, f32[3,64,8,256]{3,2,1,0:T(8,128)}, u32[]{:S(2)}) %copy-start) | copy-done | bytes 1572888
  2.0 26.4 %exchange.1 = (f32[9,64,8,256]{3,2,1,0:T(8,128)S(1)}, f32[9,64,8,256]{3,2,1,0:T(8,128)S(1)}, f32[18,8,256]{2,1,0:T(8,128)S(1)}) custom-call(f32[3,64,8,256]{3,2,1,0:T(8,128)S(1)} %copy-done), custom_call_target="tpu_custom_call" | custom-call | tf_op jit(solution)/shard_map/exchange/pallas_call | solution.py:311
  28.4 3.8 %write.1 = (f32[9,64,8,256]{3,2,1,0:T(8,128)}, f32[9,64,8,256]{3,2,1,0:T(8,128)}) custom-call(f32[9,64,8,256]{3,2,1,0:T(8,128)S(1)} %get-tuple-element.5.local_ref, f32[9,64,8,256]{3,2,1,0:T(8,128)S(1)} %get-tuple-element.6.deriv_ref, f32[18,8,256]{2,1,0:T(8,128)S(1)} %get-tuple-element.7.carry_ref), custom_call_target="tpu_custom_call" | custom-call | tf_op jit(solution)/shard_map/write/pallas_call | solution.py:337
Async XLA Ops:
  0.6 1.4 %copy-start = (f32[3,64,8,256]{3,2,1,0:T(8,128)S(1)}, f32[3,64,8,256]{3,2,1,0:T(8,128)}, u32[]{:S(2)}) copy-start(f32[3,64,8,256]{3,2,1,0:T(8,128)} %v_hbm.1) | copy-start | bytes 4718596

commit v2 on v1

v2 whole, which is shorter than its diff:
```python
import functools
import math

import jax
import jax.numpy as jnp
from jax import lax
from jax.experimental import pallas as pl
from jax.experimental.pallas import tpu as pltpu
from jax.sharding import PartitionSpec as P

MESH = pl.DeviceIdType.MESH
F32 = jnp.float32
GROUP = 8
CHUNKS = 8
HALO = 3
DERIV = (45.0 / 60.0, -9.0 / 60.0, 1.0 / 60.0)


def decay_of(stiffness):
    half = 0.5 / math.sqrt(stiffness)
    return math.exp(-2.0 * math.asinh(half)), 1.0 / math.sqrt(1.0 + 4.0 * stiffness)


def fields_of(a, b):
    return (
        a[0],
        a[1],
        a[2],
        a[0] * b[0],
        a[0] * b[1],
        a[0] * b[2],
        a[1] * b[1],
        a[1] * b[2],
        a[2] * b[2],
    )


def by_row(index, values):
    out = jnp.full(index.shape, values[0], F32)
    for i, value in enumerate(values[1:], 1):
        out = jnp.where(index == i, F32(value), out)
    return out


def vertical(center, halo, rows):
    total = None
    for k, coef in enumerate(DERIV, 1):
        upper = [
            pltpu.roll(jnp.where(rows >= k, c, h), 8 - k, 0) for c, h in zip(center, halo)
        ]
        lower = [
            pltpu.roll(jnp.where(rows < 8 - k, c, h), k, 0) for c, h in zip(center, halo)
        ]
        above = fields_of([F32(coef) * a for a in upper], upper)
        below = fields_of([F32(coef) * b for b in lower], lower)
        term = [a - b for a, b in zip(above, below)]
        total = term if total is None else [t + s for t, s in zip(total, term)]
    return total


def exchange_kernel(
    decay,
    scale,
    cells,
    blocks,
    v_hbm,
    local_ref,
    deriv_ref,
    carry_ref,
    v_ref,
    halo_ref,
    sums_ref,
    group_ref,
    total_ref,
    ring_ref,
    scan_ref,
    back_ref,
    load_sem,
    halo_send,
    halo_recv,
    send_sem,
    recv_sem,
    group_go,
    y_go,
    z_go,
):
    me = lax.axis_index("gx")
    y = lax.axis_index("gz")
    y_parts = lax.axis_size("gz")
    ring = blocks // GROUP
    z = me // GROUP
    p = lax.rem(me, GROUP)
    above_id = lax.rem(y + 1, y_parts)
    below_id = lax.rem(y + y_parts - 1, y_parts)
    wide = cells // CHUNKS
    rho = decay**cells
    jump = rho**GROUP

    def signal(sem, **device):
        pl.semaphore_signal(sem, inc=1, device_id=device, device_id_type=MESH)

    def in_group(k):
        return lax.rem(p + k, GROUP)

    def group_peer(k):
        return z * GROUP + in_group(k)

    def ring_peer(k):
        return lax.rem(z + k, ring) * GROUP + p

    barrier = pltpu.get_barrier_semaphore()
    even = lax.rem(p, 2) == 0
    for k in range(1, GROUP):

        @pl.when(lax.rem(p + k, 2) == 0)
        def _(k=k):
            signal(barrier, gx=group_peer(k))

    def load(n):
        part = pl.ds(n * wide, wide)
        return pltpu.make_async_copy(v_hbm.at[:, part], v_ref.at[:, part], load_sem.at[n])

    for n in range(CHUNKS):
        load(n).start()

    def halo(n, side):
        first, target = ((0, below_id), (8 - HALO, above_id))[side]
        part = pl.ds(n * wide, wide)
        layers = pl.ds(first, HALO)
        return pltpu.make_async_remote_copy(
            src_ref=v_hbm.at[:, part, layers],
            dst_ref=halo_ref.at[:, part, layers],
            send_sem=halo_send.at[n, side],
            recv_sem=halo_recv.at[n, side],
            device_id={"gz": target},
            device_id_type=MESH,
        )

    shape = v_ref.shape[2:]
    rows = lax.broadcasted_iota(jnp.int32, shape, 0)
    zero = jnp.zeros(shape, F32)

    def velocity(x):
        return [v_ref[c, x] for c in range(3)]

    def scaled_fields(x):
        v = velocity(x)
        return fields_of([F32(scale) * a for a in v], v)

    def forward(n, state):
        load(n).wait()
        ahead, back, weight = state
        for u in range(wide):
            x = n * wide + u
            f = scaled_fields(x)
            ahead = [F32(decay) * a + b for a, b in zip(ahead, f)]
            back = [a + weight * b for a, b in zip(back, f)]
            weight = weight * F32(decay)
            for i in range(9):
                local_ref[i, x] = ahead[i]
        return tuple(ahead), tuple(back), weight

    state = ((zero,) * 9, (zero,) * 9, jnp.ones(shape, F32))
    state = lax.fori_loop(0, CHUNKS, forward, state)
    for i in range(9):
        sums_ref[i] = state[0][i]
        sums_ref[9 + i] = state[1][i]

    def exchange(stage, source, target, peer_of, source_row, target_row, order):
        copies = []
        for k in order:
            copies.append(
                pltpu.make_async_remote_copy(
                    src_ref=source.at[:, pl.ds(source_row(k), 1)],
                    dst_ref=target.at[:, pl.ds(target_row, 1)],
                    send_sem=send_sem.at[stage, k],
                    recv_sem=recv_sem.at[stage, k],
                    device_id={"gx": peer_of(k)},
                    device_id_type=MESH,
                )
            )
        for copy in copies:
            copy.start()
        return copies

    group_order = range(1, GROUP)
    ring_order = sorted(range(1, ring), key=lambda k: -min(k, ring - k))

    @pl.when(even)
    def _():
        pl.semaphore_wait(barrier, GROUP - 1)
        signal(group_go, gx=me + 1)

    @pl.when(jnp.logical_not(even))
    def _():
        pl.semaphore_wait(group_go, 1)

    first = exchange(0, sums_ref, group_ref, group_peer, in_group, p, group_order)

    @pl.when(p == 0)
    def _():
        for other in (above_id, below_id):
            signal(barrier, gx=me + 1, gz=other)

    @pl.when(p == 2)
    def _():
        for k in range(1, ring):
            signal(barrier, gx=ring_peer(k) + 1)

    def backward(n, behind):
        for u in range(wide):
            x = cells - 1 - (n * wide + u)
            for i in range(9):
                local_ref[i, x] = local_ref[i, x] + behind[i]
            f = scaled_fields(x)
            behind = [F32(decay) * (a + b) for a, b in zip(behind, f)]
        return tuple(behind)

    lax.fori_loop(0, CHUNKS, backward, (zero,) * 9)

    def gather(collector, count, go):
        @pl.when(p == collector)
        def _():
            pl.semaphore_wait(barrier, count)
            for k in range(1, GROUP):
                signal(go, gx=group_peer(k))

        @pl.when(p != collector)
        def _():
            pl.semaphore_wait(go, 1)

    gather(1, 2, y_go)
    for n in range(CHUNKS):
        for side in range(2):
            halo(n, side).start()

    def derive(n, _):
        halo(n, 0).wait_recv()
        halo(n, 1).wait_recv()

        def one(j, _):
            x = n * wide + j
            out = vertical(velocity(x), [halo_ref[c, x] for c in range(3)], rows)
            for i in range(9):
                deriv_ref[i, x] = out[i]
            return 0

        return lax.fori_loop(0, wide, one, 0)

    rising = by_row(rows, [rho**b for b in range(GROUP)])
    sinking = by_row(rows, [rho ** (GROUP - 1 - b) for b in range(GROUP)])
    mine = rows == p
    for copy in first:
        copy.wait_recv()
    for i in range(18):
        held = jnp.where(mine, sums_ref[i], group_ref[i])
        group_ref[i] = held
        part = held * (sinking if i < 9 else rising)
        total_ref[i] = jnp.broadcast_to(jnp.sum(part, axis=0, keepdims=True), shape)

    gather(3, ring - 1, z_go)
    second = exchange(1, total_ref, ring_ref, ring_peer, lambda k: z, z, ring_order)

    for i in range(18):
        if i < 9:
            run = jnp.where(rows >= 1, pltpu.roll(group_ref[i], 1, 0), F32(0))
            for s in (1, 2, 4):
                moved = jnp.where(rows >= s, pltpu.roll(run, s, 0), F32(0))
                run = run + F32(rho**s) * moved
        else:
            run = jnp.where(rows < 7, pltpu.roll(group_ref[i], 7, 0), F32(0))
            for s in (1, 2, 4):
                moved = jnp.where(rows < 8 - s, pltpu.roll(run, 8 - s, 0), F32(0))
                run = run + F32(rho**s) * moved
        scan_ref[i] = run

    closed = 1.0 / (1.0 - jump**ring)
    powers = [closed * jump**e for e in range(ring)]
    ahead_weight = by_row(lax.rem(z - rows + 2 * ring - 1, ring), powers)
    back_weight = by_row(lax.rem(rows - z + 2 * ring - 1, ring), powers)
    own = rows == z
    for copy in second:
        copy.wait_recv()
    for i in range(18):
        held = jnp.where(own, total_ref[i], ring_ref[i])
        part = held * (ahead_weight if i < 9 else back_weight)
        entering = jnp.broadcast_to(jnp.sum(part, axis=0, keepdims=True), shape)
        scan_ref[i] = scan_ref[i] + (rising if i < 9 else sinking) * entering

    third = exchange(2, scan_ref, back_ref, group_peer, in_group, p, group_order)

    lax.fori_loop(0, CHUNKS, derive, 0)

    for copy in third:
        copy.wait_recv()
    for i in range(18):
        carry_ref[i] = jnp.where(mine, scan_ref[i], back_ref[i])

    for copy in first + second + third:
        copy.wait_send()
    for n in range(CHUNKS):
        for side in range(2):
            halo(n, side).wait_send()


def write_kernel(decay, cells, local_ref, deriv_ref, carry_ref, out_s, out_d, held, sem_s, sem_d):
    wide = cells // CHUNKS

    def put_d(n):
        part = pl.ds(n * wide, wide)
        return pltpu.make_async_copy(deriv_ref.at[:, part], out_d.at[:, part], sem_d.at[n])

    def put_s(n):
        part = pl.ds(n * wide, wide)
        return pltpu.make_async_copy(held.at[:, part], out_s.at[:, part], sem_s.at[n])

    for n in range(CHUNKS):
        put_d(n).start()

    def correct(n, weights):
        rising, falling = weights
        for u in range(wide):
            x = n * wide + u
            up = rising * F32(decay ** (u + 1))
            down = falling * F32(decay ** (wide - u))
            for i in range(9):
                held[i, x] = local_ref[i, x] + (up * carry_ref[i] + down * carry_ref[9 + i])
        put_s(n).start()
        return rising * F32(decay**wide), falling * F32(decay**-wide)

    shape = carry_ref.shape[1:]
    ones = jnp.ones(shape, F32)
    lax.fori_loop(0, CHUNKS, correct, (ones, ones * F32(decay ** (cells - wide))))
    for n in range(CHUNKS):
        put_d(n).wait()
        put_s(n).wait()


def shards(velocity):
    comps, cells, layers, span = velocity.shape
    blocks = lax.axis_size("gx")
    ring = blocks // GROUP
    decay, scale = decay_of((cells * blocks / 8.0) ** 2)
    big = (9, cells, layers, span)
    small = (18, layers, span)
    local, deriv, carry = pl.pallas_call(
        functools.partial(exchange_kernel, decay, scale, cells, blocks),
        out_shape=(
            pltpu.VMEM(big, F32),
            pltpu.VMEM(big, F32),
            pltpu.VMEM(small, F32),
        ),
        in_specs=[pl.BlockSpec(memory_space=pl.ANY)],
        out_specs=[pl.BlockSpec(memory_space=pltpu.VMEM)] * 3,
        scratch_shapes=[
            pltpu.VMEM((comps, cells, layers, span), F32),
            pltpu.VMEM((comps, cells, layers, span), F32),
        ]
        + [pltpu.VMEM(small, F32)] * 6
        + [
            pltpu.SemaphoreType.DMA((CHUNKS,)),
            pltpu.SemaphoreType.DMA((CHUNKS, 2)),
            pltpu.SemaphoreType.DMA((CHUNKS, 2)),
            pltpu.SemaphoreType.DMA((3, GROUP)),
            pltpu.SemaphoreType.DMA((3, GROUP)),
            pltpu.SemaphoreType.REGULAR,
            pltpu.SemaphoreType.REGULAR,
            pltpu.SemaphoreType.REGULAR,
        ],
        compiler_params=pltpu.CompilerParams(
            collective_id=0, has_side_effects=True, vmem_limit_bytes=44 << 20
        ),
        name="exchange",
    )(velocity)
    return pl.pallas_call(
        functools.partial(write_kernel, decay, cells),
        out_shape=(jax.ShapeDtypeStruct(big, F32), jax.ShapeDtypeStruct(big, F32)),
        in_specs=[pl.BlockSpec(memory_space=pltpu.VMEM)] * 3,
        out_specs=[pl.BlockSpec(memory_space=pltpu.HBM)] * 2,
        scratch_shapes=[
            pltpu.VMEM(big, F32),
            pltpu.SemaphoreType.DMA((CHUNKS,)),
            pltpu.SemaphoreType.DMA((CHUNKS,)),
        ],
        compiler_params=pltpu.CompilerParams(vmem_limit_bytes=24 << 20),
        name="write",
    )(local, deriv, carry)


def solution(mesh):
    spec = P(None, "gx", "gz", None)
    return jax.shard_map(
        shards, mesh=mesh, in_specs=(spec,), out_specs=(spec, spec), check_vma=False
    )
```

time: 32.3 us -> 29.3 us (0.907)
  Pallas kernels: 30.2 us -> 28.6 us
  local copies, waits for them, and re-layouts: 1.4 us -> 0 us
    pallas_call x1, Pallas kernels: 26.4 us -> 24.8 us  [shards(): pl.pallas_call(functools.partial(exchange_kernel, decay, scale, cells, bl...]
    unnamed x2 -> x0, local copies, waits for them, and re-layouts: 1.4 us -> none
where the time goes in v2:
time: 29.3 us; the launch traced here: 29.2 us
  Pallas kernels  28.6 us (98%)
  between operations  0.64 us (2%)
    pallas_call x1, Pallas kernels, shards(): pl.pallas_call(functools.partial(exchange_kernel, decay, scale, cells, bl...  24.8 us
    pallas_call x1, Pallas kernels, shards(): pl.pallas_call(functools.partial(write_kernel, decay, cells), out_shape=(...  3.75 us

profile of v2, /device:TPU:1, one launch (start us, length us, event | category | flops | bytes accessed | tf_op | source)
XLA Modules:
  0.0 29.2 jit_solution(3272035128430690558)
XLA Ops:
  0.6 24.8 %exchange.1 = (f32[9,64,8,256]{3,2,1,0:T(8,128)S(1)}, f32[9,64,8,256]{3,2,1,0:T(8,128)S(1)}, f32[18,8,256]{2,1,0:T(8,128)S(1)}) custom-call(f32[3,64,8,256]{3,2,1,0:T(8,128)} %v_hbm.1), custom_call_target="tpu_custom_call" | custom-call | tf_op jit(solution)/shard_map/exchange/pallas_call | solution.py:346
  25.5 3.8 %write.1 = (f32[9,64,8,256]{3,2,1,0:T(8,128)}, f32[9,64,8,256]{3,2,1,0:T(8,128)}) custom-call(f32[9,64,8,256]{3,2,1,0:T(8,128)S(1)} %get-tuple-element.5.local_ref, f32[9,64,8,256]{3,2,1,0:T(8,128)S(1)} %get-tuple-element.6.deriv_ref, f32[18,8,256]{2,1,0:T(8,128)S(1)} %get-tuple-element.7.carry_ref), custom_call_target="tpu_custom_call" | custom-call | tf_op jit(solution)/shard_map/write/pallas_call | solution.py:375

commit v3 on v2

--- a/solution.py
+++ b/solution.py
@@ -116,6 +116,17 @@
         def _(k=k):
             signal(barrier, gx=group_peer(k))
 
+    second_chip = p // 2 == 1
+    for other in (above_id, below_id):
+
+        @pl.when(second_chip)
+        def _(other=other):
+            signal(barrier, gx=z * GROUP + 1, gz=other)
+
+        @pl.when(jnp.logical_not(second_chip))
+        def _(other=other):
+            signal(barrier, gx=me + 1 - lax.rem(p, 2), gz=other)
+
     def load(n):
         part = pl.ds(n * wide, wide)
         return pltpu.make_async_copy(v_hbm.at[:, part], v_ref.at[:, part], load_sem.at[n])
@@ -183,8 +194,7 @@
             copy.start()
         return copies
 
-    group_order = range(1, GROUP)
-    ring_order = sorted(range(1, ring), key=lambda k: -min(k, ring - k))
+    group_order = sorted(range(1, GROUP), key=lambda k: abs(k - GROUP // 2))
 
     @pl.when(even)
     def _():
@@ -195,17 +205,31 @@
     def _():
         pl.semaphore_wait(group_go, 1)
 
-    first = exchange(0, sums_ref, group_ref, group_peer, in_group, p, group_order)
-
-    @pl.when(p == 0)
-    def _():
-        for other in (above_id, below_id):
-            signal(barrier, gx=me + 1, gz=other)
-
     @pl.when(p == 2)
     def _():
         for k in range(1, ring):
             signal(barrier, gx=ring_peer(k) + 1)
+
+    first = exchange(0, sums_ref, group_ref, group_peer, in_group, p, group_order)
+
+    @pl.when(p == 1)
+    def _():
+        pl.semaphore_wait(barrier, 8)
+        for target in (me - 1, me + 1, me + 2):
+            signal(y_go, gx=target)
+
+    @pl.when(jnp.logical_and(jnp.logical_not(even), p >= 5))
+    def _():
+        pl.semaphore_wait(barrier, 4)
+        signal(y_go, gx=me - 1)
+
+    @pl.when(jnp.logical_or(even, p == 3))
+    def _():
+        pl.semaphore_wait(y_go, 1)
+
+    for n in range(CHUNKS):
+        for side in range(2):
+            halo(n, side).start()
 
     def backward(n, behind):
         for u in range(wide):
@@ -218,21 +242,11 @@
 
     lax.fori_loop(0, CHUNKS, backward, (zero,) * 9)
 
-    def gather(collector, count, go):
-        @pl.when(p == collector)
-        def _():
-            pl.semaphore_wait(barrier, count)
-            for k in range(1, GROUP):
-                signal(go, gx=group_peer(k))
-
-        @pl.when(p != collector)
-        def _():
-            pl.semaphore_wait(go, 1)
-
-    gather(1, 2, y_go)
-    for n in range(CHUNKS):
-        for side in range(2):
-            halo(n, side).start()
+    @pl.when(p == 3)
+    def _():
+        pl.semaphore_wait(barrier, ring - 1)
+        for k in range(1, GROUP):
+            signal(z_go, gx=group_peer(k))
 
     def derive(n, _):
         halo(n, 0).wait_recv()
@@ -258,8 +272,24 @@
         part = held * (sinking if i < 9 else rising)
         total_ref[i] = jnp.broadcast_to(jnp.sum(part, axis=0, keepdims=True), shape)
 
-    gather(3, ring - 1, z_go)
-    second = exchange(1, total_ref, ring_ref, ring_peer, lambda k: z, z, ring_order)
+    @pl.when(p != 3)
+    def _():
+        pl.semaphore_wait(z_go, 1)
+
+    def total_copy(target, sent, received):
+        return pltpu.make_async_remote_copy(
+            src_ref=total_ref.at[:, pl.ds(z, 1)],
+            dst_ref=ring_ref.at[:, pl.ds(z, 1)],
+            send_sem=send_sem.at[1, sent],
+            recv_sem=recv_sem.at[1, received],
+            device_id={"gx": target * GROUP + p},
+            device_id_type=MESH,
+        )
+
+    second = [total_copy(0, j, j) for j in range(ring - 1)]
+    for j in range(ring - 1):
+        target = j + (j + ring - z) // ring
+        total_copy(target, j, z - 1 + (target + ring - z) // ring).start()
 
     for i in range(18):
         if i < 9:

time: 29.3 us -> 27 us (0.922)
  Pallas kernels: 28.6 us -> 26.2 us
    pallas_call x1, Pallas kernels: 24.8 us -> 22.5 us  [shards(): pl.pallas_call(functools.partial(exchange_kernel, decay, scale, cells, bl...]
where the time goes in v3:
time: 27 us; the launch traced here: 26.9 us
  Pallas kernels  26.2 us (97%)
  between operations  0.64 us (2%)
    pallas_call x1, Pallas kernels, shards(): pl.pallas_call(functools.partial(exchange_kernel, decay, scale, cells, bl...  22.5 us
    pallas_call x1, Pallas kernels, shards(): pl.pallas_call(functools.partial(write_kernel, decay, cells), out_shape=(...  3.75 us

profile of v3, /device:TPU:1, one launch (start us, length us, event | category | flops | bytes accessed | tf_op | source)
XLA Modules:
  0.0 26.9 jit_solution(11197338060305017224)
XLA Ops:
  0.6 22.5 %exchange.1 = (f32[9,64,8,256]{3,2,1,0:T(8,128)S(1)}, f32[9,64,8,256]{3,2,1,0:T(8,128)S(1)}, f32[18,8,256]{2,1,0:T(8,128)S(1)}) custom-call(f32[3,64,8,256]{3,2,1,0:T(8,128)} %v_hbm.1), custom_call_target="tpu_custom_call" | custom-call | tf_op jit(solution)/shard_map/exchange/pallas_call | solution.py:376
  23.1 3.8 %write.1 = (f32[9,64,8,256]{3,2,1,0:T(8,128)}, f32[9,64,8,256]{3,2,1,0:T(8,128)}) custom-call(f32[9,64,8,256]{3,2,1,0:T(8,128)S(1)} %get-tuple-element.5.local_ref, f32[9,64,8,256]{3,2,1,0:T(8,128)S(1)} %get-tuple-element.6.deriv_ref, f32[18,8,256]{2,1,0:T(8,128)S(1)} %get-tuple-element.7.carry_ref), custom_call_target="tpu_custom_call" | custom-call | tf_op jit(solution)/shard_map/write/pallas_call | solution.py:405

commit v4 on v3

--- a/solution.py
+++ b/solution.py
@@ -12,7 +12,10 @@
 F32 = jnp.float32
 GROUP = 8
 CHUNKS = 8
+PIECES = 8
 HALO = 3
+ORDER1 = (0, 7, 1, 6, 2, 5, 3, 4)
+ORDER3 = (1, 0, 7, 6, 2, 3, 4, 5)
 DERIV = (45.0 / 60.0, -9.0 / 60.0, 1.0 / 60.0)
 
 
@@ -141,9 +144,20 @@
         return pltpu.make_async_remote_copy(
             src_ref=v_hbm.at[:, part, layers],
             dst_ref=halo_ref.at[:, part, layers],
-            send_sem=halo_send.at[n, side],
-            recv_sem=halo_recv.at[n, side],
+            send_sem=halo_send,
+            recv_sem=halo_recv.at[n],
             device_id={"gz": target},
+            device_id_type=MESH,
+        )
+
+    def both_halos(part, received):
+        layers = pl.ds(0, 2 * HALO)
+        return pltpu.make_async_remote_copy(
+            src_ref=v_hbm.at[:, part, layers],
+            dst_ref=halo_ref.at[:, part, layers],
+            send_sem=halo_send,
+            recv_sem=received,
+            device_id={"gz": above_id},
             device_id_type=MESH,
         )
 
@@ -177,24 +191,37 @@
         sums_ref[i] = state[0][i]
         sums_ref[9 + i] = state[1][i]
 
-    def exchange(stage, source, target, peer_of, source_row, target_row, order):
-        copies = []
-        for k in order:
-            copies.append(
-                pltpu.make_async_remote_copy(
-                    src_ref=source.at[:, pl.ds(source_row(k), 1)],
-                    dst_ref=target.at[:, pl.ds(target_row, 1)],
-                    send_sem=send_sem.at[stage, k],
-                    recv_sem=recv_sem.at[stage, k],
-                    device_id={"gx": peer_of(k)},
-                    device_id_type=MESH,
-                )
-            )
-        for copy in copies:
-            copy.start()
-        return copies
-
-    group_order = sorted(range(1, GROUP), key=lambda k: abs(k - GROUP // 2))
+    def carries(stage, source, target, source_rows, target_rows, peer):
+        return pltpu.make_async_remote_copy(
+            src_ref=source.at[:, source_rows],
+            dst_ref=target.at[:, target_rows],
+            send_sem=send_sem.at[stage],
+            recv_sem=recv_sem.at[stage],
+            device_id={"gx": peer},
+            device_id_type=MESH,
+        )
+
+    def all_carries(stage, source, target, count):
+        every = pl.ds(0, count - 1)
+        return carries(stage, source, target, every, every, me)
+
+    def others(own, order, act):
+        for to in order:
+
+            @pl.when(own != to)
+            def _(to=to):
+                act(to)
+
+    def start_group(stage, source, target, order):
+        def start(to):
+            peer = z * GROUP + to
+            carries(stage, source, target, pl.ds(to, 1), pl.ds(p, 1), peer).start()
+
+        others(p, order, start)
+
+    first = all_carries(0, sums_ref, group_ref, GROUP)
+    second = all_carries(1, total_ref, ring_ref, ring)
+    third = all_carries(2, scan_ref, back_ref, GROUP)
 
     @pl.when(even)
     def _():
@@ -210,7 +237,7 @@
         for k in range(1, ring):
             signal(barrier, gx=ring_peer(k) + 1)
 
-    first = exchange(0, sums_ref, group_ref, group_peer, in_group, p, group_order)
+    start_group(0, sums_ref, group_ref, ORDER1)
 
     @pl.when(p == 1)
     def _():
@@ -240,8 +267,6 @@
             behind = [F32(decay) * (a + b) for a, b in zip(behind, f)]
         return tuple(behind)
 
-    lax.fori_loop(0, CHUNKS, backward, (zero,) * 9)
-
     @pl.when(p == 3)
     def _():
         pl.semaphore_wait(barrier, ring - 1)
@@ -249,8 +274,7 @@
             signal(z_go, gx=group_peer(k))
 
     def derive(n, _):
-        halo(n, 0).wait_recv()
-        halo(n, 1).wait_recv()
+        both_halos(pl.ds(n * wide, wide), halo_recv.at[n]).wait_recv()
 
         def one(j, _):
             x = n * wide + j
@@ -264,8 +288,7 @@
     rising = by_row(rows, [rho**b for b in range(GROUP)])
     sinking = by_row(rows, [rho ** (GROUP - 1 - b) for b in range(GROUP)])
     mine = rows == p
-    for copy in first:
-        copy.wait_recv()
+    first.wait_recv()
     for i in range(18):
         held = jnp.where(mine, sums_ref[i], group_ref[i])
         group_ref[i] = held
@@ -276,21 +299,14 @@
     def _():
         pl.semaphore_wait(z_go, 1)
 
-    def total_copy(target, sent, received):
-        return pltpu.make_async_remote_copy(
-            src_ref=total_ref.at[:, pl.ds(z, 1)],
-            dst_ref=ring_ref.at[:, pl.ds(z, 1)],
-            send_sem=send_sem.at[1, sent],
-            recv_sem=recv_sem.at[1, received],
-            device_id={"gx": target * GROUP + p},
-            device_id_type=MESH,
-        )
-
-    second = [total_copy(0, j, j) for j in range(ring - 1)]
-    for j in range(ring - 1):
-        target = j + (j + ring - z) // ring
-        total_copy(target, j, z - 1 + (target + ring - z) // ring).start()
-
+    def start_ring(*planes):
+        def start(to):
+            peer = to * GROUP + p
+            carries(1, total_ref, ring_ref, pl.ds(z, 1), pl.ds(z, 1), peer).start()
+
+        others(z, planes, start)
+
+    start_ring(0)
     for i in range(18):
         if i < 9:
             run = jnp.where(rows >= 1, pltpu.roll(group_ref[i], 1, 0), F32(0))
@@ -304,47 +320,50 @@
                 run = run + F32(rho**s) * moved
         scan_ref[i] = run
 
+    start_ring(1)
+    half = CHUNKS // 2
+    behind = lax.fori_loop(0, half, backward, (zero,) * 9)
+    start_ring(2, 3)
+    lax.fori_loop(half, CHUNKS, backward, behind)
+    start_ring(*range(4, ring))
+
     closed = 1.0 / (1.0 - jump**ring)
     powers = [closed * jump**e for e in range(ring)]
     ahead_weight = by_row(lax.rem(z - rows + 2 * ring - 1, ring), powers)
     back_weight = by_row(lax.rem(rows - z + 2 * ring - 1, ring), powers)
     own = rows == z
-    for copy in second:
-        copy.wait_recv()
+    second.wait_recv()
     for i in range(18):
         held = jnp.where(own, total_ref[i], ring_ref[i])
         part = held * (ahead_weight if i < 9 else back_weight)
         entering = jnp.broadcast_to(jnp.sum(part, axis=0, keepdims=True), shape)
         scan_ref[i] = scan_ref[i] + (rising if i < 9 else sinking) * entering
 
-    third = exchange(2, scan_ref, back_ref, group_peer, in_group, p, group_order)
+    start_group(2, scan_ref, back_ref, ORDER3)
 
     lax.fori_loop(0, CHUNKS, derive, 0)
 
-    for copy in third:
-        copy.wait_recv()
+    third.wait_recv()
     for i in range(18):
         carry_ref[i] = jnp.where(mine, scan_ref[i], back_ref[i])
 
-    for copy in first + second + third:
+    for copy in (first, second, third):
         copy.wait_send()
-    for n in range(CHUNKS):
-        for side in range(2):
-            halo(n, side).wait_send()
+    both_halos(pl.ds(0, cells), halo_recv.at[0]).wait_send()
 
 
 def write_kernel(decay, cells, local_ref, deriv_ref, carry_ref, out_s, out_d, held, sem_s, sem_d):
-    wide = cells // CHUNKS
+    wide = cells // PIECES
 
     def put_d(n):
         part = pl.ds(n * wide, wide)
-        return pltpu.make_async_copy(deriv_ref.at[:, part], out_d.at[:, part], sem_d.at[n])
+        return pltpu.make_async_copy(deriv_ref.at[:, part], out_d.at[:, part], sem_d)
 
     def put_s(n):
         part = pl.ds(n * wide, wide)
-        return pltpu.make_async_copy(held.at[:, part], out_s.at[:, part], sem_s.at[n])
-
-    for n in range(CHUNKS):
+        return pltpu.make_async_copy(held.at[:, part], out_s.at[:, part], sem_s)
+
+    for n in range(PIECES):
         put_d(n).start()
 
     def correct(n, weights):
@@ -360,10 +379,9 @@
 
     shape = carry_ref.shape[1:]
     ones = jnp.ones(shape, F32)
-    lax.fori_loop(0, CHUNKS, correct, (ones, ones * F32(decay ** (cells - wide))))
-    for n in range(CHUNKS):
-        put_d(n).wait()
-        put_s(n).wait()
+    lax.fori_loop(0, PIECES, correct, (ones, ones * F32(decay ** (cells - wide))))
+    pltpu.make_async_copy(deriv_ref, out_d, sem_d).wait()
+    pltpu.make_async_copy(held, out_s, sem_s).wait()
 
 
 def shards(velocity):
@@ -389,10 +407,10 @@
         + [pltpu.VMEM(small, F32)] * 6
         + [
             pltpu.SemaphoreType.DMA((CHUNKS,)),
-            pltpu.SemaphoreType.DMA((CHUNKS, 2)),
-            pltpu.SemaphoreType.DMA((CHUNKS, 2)),
-            pltpu.SemaphoreType.DMA((3, GROUP)),
-            pltpu.SemaphoreType.DMA((3, GROUP)),
+            pltpu.SemaphoreType.DMA,
+            pltpu.SemaphoreType.DMA((CHUNKS,)),
+            pltpu.SemaphoreType.DMA((3,)),
+            pltpu.SemaphoreType.DMA((3,)),
             pltpu.SemaphoreType.REGULAR,
             pltpu.SemaphoreType.REGULAR,
             pltpu.SemaphoreType.REGULAR,
@@ -409,8 +427,8 @@
         out_specs=[pl.BlockSpec(memory_space=pltpu.HBM)] * 2,
         scratch_shapes=[
             pltpu.VMEM(big, F32),
-            pltpu.SemaphoreType.DMA((CHUNKS,)),
-            pltpu.SemaphoreType.DMA((CHUNKS,)),
+            pltpu.SemaphoreType.DMA,
+            pltpu.SemaphoreType.DMA,
         ],
         compiler_params=pltpu.CompilerParams(vmem_limit_bytes=24 << 20),
         name="write",

time: 27 us -> 26.1 us (0.967)
  Pallas kernels: 26.2 us -> 25.4 us
    pallas_call x1, Pallas kernels: 22.5 us -> 21.8 us  [shards(): pl.pallas_call(functools.partial(exchange_kernel, decay, scale, cells, bl...]
where the time goes in v4:
time: 26.1 us; the launch traced here: 26 us
  Pallas kernels  25.4 us (97%)
  between operations  0.64 us (2%)
    pallas_call x1, Pallas kernels, shards(): pl.pallas_call(functools.partial(exchange_kernel, decay, scale, cells, bl...  21.8 us
    pallas_call x1, Pallas kernels, shards(): pl.pallas_call(functools.partial(write_kernel, decay, cells), out_shape=(...  3.63 us

profile of v4, /device:TPU:1, one launch (start us, length us, event | category | flops | bytes accessed | tf_op | source)
XLA Modules:
  0.0 26.0 jit_solution(10087897627458736044)
XLA Ops:
  0.6 21.8 %exchange.1 = (f32[9,64,8,256]{3,2,1,0:T(8,128)S(1)}, f32[9,64,8,256]{3,2,1,0:T(8,128)S(1)}, f32[18,8,256]{2,1,0:T(8,128)S(1)}) custom-call(f32[3,64,8,256]{3,2,1,0:T(8,128)} %v_hbm.1), custom_call_target="tpu_custom_call" | custom-call | tf_op jit(solution)/shard_map/exchange/pallas_call | solution.py:394
  22.4 3.6 %write.1 = (f32[9,64,8,256]{3,2,1,0:T(8,128)}, f32[9,64,8,256]{3,2,1,0:T(8,128)}) custom-call(f32[9,64,8,256]{3,2,1,0:T(8,128)S(1)} %get-tuple-element.5.local_ref, f32[9,64,8,256]{3,2,1,0:T(8,128)S(1)} %get-tuple-element.6.deriv_ref, f32[18,8,256]{2,1,0:T(8,128)S(1)} %get-tuple-element.7.carry_ref), custom_call_target="tpu_custom_call" | custom-call | tf_op jit(solution)/shard_map/write/pallas_call | solution.py:423

commit v5 on v4

--- a/solution.py
+++ b/solution.py
@@ -13,6 +13,7 @@
 GROUP = 8
 CHUNKS = 8
 PIECES = 8
+PARTS = (32, 16, 8, 8)
 HALO = 3
 ORDER1 = (0, 7, 1, 6, 2, 5, 3, 4)
 ORDER3 = (1, 0, 7, 6, 2, 3, 4, 5)
@@ -139,7 +140,7 @@
 
     def halo(n, side):
         first, target = ((0, below_id), (8 - HALO, above_id))[side]
-        part = pl.ds(n * wide, wide)
+        part = pl.ds(sum(PARTS[:n]), PARTS[n])
         layers = pl.ds(first, HALO)
         return pltpu.make_async_remote_copy(
             src_ref=v_hbm.at[:, part, layers],
@@ -185,6 +186,12 @@
                 local_ref[i, x] = ahead[i]
         return tuple(ahead), tuple(back), weight
 
+    def pass_on():
+        pl.semaphore_wait(barrier, GROUP - 1)
+        signal(group_go, gx=me + 1)
+
+    pl.when(jnp.logical_and(even, p >= GROUP // 2))(pass_on)
+
     state = ((zero,) * 9, (zero,) * 9, jnp.ones(shape, F32))
     state = lax.fori_loop(0, CHUNKS, forward, state)
     for i in range(9):
@@ -223,10 +230,7 @@
     second = all_carries(1, total_ref, ring_ref, ring)
     third = all_carries(2, scan_ref, back_ref, GROUP)
 
-    @pl.when(even)
-    def _():
-        pl.semaphore_wait(barrier, GROUP - 1)
-        signal(group_go, gx=me + 1)
+    pl.when(jnp.logical_and(even, p < GROUP // 2))(pass_on)
 
     @pl.when(jnp.logical_not(even))
     def _():
@@ -254,7 +258,7 @@
     def _():
         pl.semaphore_wait(y_go, 1)
 
-    for n in range(CHUNKS):
+    for n in range(len(PARTS)):
         for side in range(2):
             halo(n, side).start()
 
@@ -273,17 +277,18 @@
         for k in range(1, GROUP):
             signal(z_go, gx=group_peer(k))
 
-    def derive(n, _):
-        both_halos(pl.ds(n * wide, wide), halo_recv.at[n]).wait_recv()
+    def derive(n):
+        start = sum(PARTS[:n])
+        both_halos(pl.ds(start, PARTS[n]), halo_recv.at[n]).wait_recv()
 
         def one(j, _):
-            x = n * wide + j
+            x = start + j
             out = vertical(velocity(x), [halo_ref[c, x] for c in range(3)], rows)
             for i in range(9):
                 deriv_ref[i, x] = out[i]
             return 0
 
-        return lax.fori_loop(0, wide, one, 0)
+        lax.fori_loop(0, PARTS[n], one, 0)
 
     rising = by_row(rows, [rho**b for b in range(GROUP)])
     sinking = by_row(rows, [rho ** (GROUP - 1 - b) for b in range(GROUP)])
@@ -341,7 +346,8 @@
 
     start_group(2, scan_ref, back_ref, ORDER3)
 
-    lax.fori_loop(0, CHUNKS, derive, 0)
+    for n in range(len(PARTS)):
+        derive(n)
 
     third.wait_recv()
     for i in range(18):
@@ -408,7 +414,7 @@
         + [
             pltpu.SemaphoreType.DMA((CHUNKS,)),
             pltpu.SemaphoreType.DMA,
-            pltpu.SemaphoreType.DMA((CHUNKS,)),
+            pltpu.SemaphoreType.DMA((len(PARTS),)),
             pltpu.SemaphoreType.DMA((3,)),
             pltpu.SemaphoreType.DMA((3,)),
             pltpu.SemaphoreType.REGULAR,

time: 26.1 us -> 26.1 us (level)
  no operation moved by 1% of the time
where the time goes in v5:
time: 26.1 us; the launch traced here: 26 us
  Pallas kernels  25.4 us (97%)
  between operations  0.64 us (2%)
    pallas_call x1, Pallas kernels, shards(): pl.pallas_call(functools.partial(exchange_kernel, decay, scale, cells, bl...  21.7 us
    pallas_call x1, Pallas kernels, shards(): pl.pallas_call(functools.partial(write_kernel, decay, cells), out_shape=(...  3.63 us

profile of v5, /device:TPU:1, one launch (start us, length us, event | category | flops | bytes accessed | tf_op | source)
XLA Modules:
  0.0 26.0 jit_solution(5554470712859784123)
XLA Ops:
  0.6 21.7 %exchange.1 = (f32[9,64,8,256]{3,2,1,0:T(8,128)S(1)}, f32[9,64,8,256]{3,2,1,0:T(8,128)S(1)}, f32[18,8,256]{2,1,0:T(8,128)S(1)}) custom-call(f32[3,64,8,256]{3,2,1,0:T(8,128)} %v_hbm.1), custom_call_target="tpu_custom_call" | custom-call | tf_op jit(solution)/shard_map/exchange/pallas_call | solution.py:400
  22.4 3.6 %write.1 = (f32[9,64,8,256]{3,2,1,0:T(8,128)}, f32[9,64,8,256]{3,2,1,0:T(8,128)}) custom-call(f32[9,64,8,256]{3,2,1,0:T(8,128)S(1)} %get-tuple-element.5.local_ref, f32[9,64,8,256]{3,2,1,0:T(8,128)S(1)} %get-tuple-element.6.deriv_ref, f32[18,8,256]{2,1,0:T(8,128)S(1)} %get-tuple-element.7.carry_ref), custom_call_target="tpu_custom_call" | custom-call | tf_op jit(solution)/shard_map/write/pallas_call | solution.py:429

commit v6 on v5

--- a/solution.py
+++ b/solution.py
@@ -15,7 +15,7 @@
 PIECES = 8
 PARTS = (32, 16, 8, 8)
 HALO = 3
-ORDER1 = (0, 7, 1, 6, 2, 5, 3, 4)
+ORDER1 = (6, 0, 4, 2, 7, 1, 5, 3)
 ORDER3 = (1, 0, 7, 6, 2, 3, 4, 5)
 DERIV = (45.0 / 60.0, -9.0 / 60.0, 1.0 / 60.0)
 
@@ -120,14 +120,14 @@
         def _(k=k):
             signal(barrier, gx=group_peer(k))
 
-    second_chip = p // 2 == 1
+    third_chip = p // 2 == 2
     for other in (above_id, below_id):
 
-        @pl.when(second_chip)
+        @pl.when(third_chip)
         def _(other=other):
-            signal(barrier, gx=z * GROUP + 1, gz=other)
-
-        @pl.when(jnp.logical_not(second_chip))
+            signal(barrier, gx=z * GROUP + 7, gz=other)
+
+        @pl.when(jnp.logical_not(third_chip))
         def _(other=other):
             signal(barrier, gx=me + 1 - lax.rem(p, 2), gz=other)
 
@@ -236,25 +236,25 @@
     def _():
         pl.semaphore_wait(group_go, 1)
 
-    @pl.when(p == 2)
+    @pl.when(p == 4)
     def _():
         for k in range(1, ring):
             signal(barrier, gx=ring_peer(k) + 1)
 
     start_group(0, sums_ref, group_ref, ORDER1)
 
-    @pl.when(p == 1)
+    @pl.when(p == 7)
     def _():
         pl.semaphore_wait(barrier, 8)
-        for target in (me - 1, me + 1, me + 2):
+        for target in (me - 1, me - 2, me - 3):
             signal(y_go, gx=target)
 
-    @pl.when(jnp.logical_and(jnp.logical_not(even), p >= 5))
+    @pl.when(jnp.logical_and(jnp.logical_not(even), p < 5))
     def _():
         pl.semaphore_wait(barrier, 4)
         signal(y_go, gx=me - 1)
 
-    @pl.when(jnp.logical_or(even, p == 3))
+    @pl.when(jnp.logical_or(even, p == 5))
     def _():
         pl.semaphore_wait(y_go, 1)
 
@@ -271,7 +271,7 @@
             behind = [F32(decay) * (a + b) for a, b in zip(behind, f)]
         return tuple(behind)
 
-    @pl.when(p == 3)
+    @pl.when(p == 5)
     def _():
         pl.semaphore_wait(barrier, ring - 1)
         for k in range(1, GROUP):
@@ -300,7 +300,7 @@
         part = held * (sinking if i < 9 else rising)
         total_ref[i] = jnp.broadcast_to(jnp.sum(part, axis=0, keepdims=True), shape)
 
-    @pl.when(p != 3)
+    @pl.when(p != 5)
     def _():
         pl.semaphore_wait(z_go, 1)
 

time: 26.1 us -> 26 us (level)
  no operation moved by 1% of the time
where the time goes in v6:
time: 26 us; the launch traced here: 25.9 us
  Pallas kernels  25.3 us (97%)
  between operations  0.64 us (2%)
    pallas_call x1, Pallas kernels, shards(): pl.pallas_call(functools.partial(exchange_kernel, decay, scale, cells, bl...  21.7 us
    pallas_call x1, Pallas kernels, shards(): pl.pallas_call(functools.partial(write_kernel, decay, cells), out_shape=(...  3.63 us

profile of v6, /device:TPU:1, one launch (start us, length us, event | category | flops | bytes accessed | tf_op | source)
XLA Modules:
  0.0 25.9 jit_solution(16723265607665653270)
XLA Ops:
  0.6 21.7 %exchange.1 = (f32[9,64,8,256]{3,2,1,0:T(8,128)S(1)}, f32[9,64,8,256]{3,2,1,0:T(8,128)S(1)}, f32[18,8,256]{2,1,0:T(8,128)S(1)}) custom-call(f32[3,64,8,256]{3,2,1,0:T(8,128)} %v_hbm.1), custom_call_target="tpu_custom_call" | custom-call | tf_op jit(solution)/shard_map/exchange/pallas_call | solution.py:400
  22.3 3.6 %write.1 = (f32[9,64,8,256]{3,2,1,0:T(8,128)}, f32[9,64,8,256]{3,2,1,0:T(8,128)}) custom-call(f32[9,64,8,256]{3,2,1,0:T(8,128)S(1)} %get-tuple-element.5.local_ref, f32[9,64,8,256]{3,2,1,0:T(8,128)S(1)} %get-tuple-element.6.deriv_ref, f32[18,8,256]{2,1,0:T(8,128)S(1)} %get-tuple-element.7.carry_ref), custom_call_target="tpu_custom_call" | custom-call | tf_op jit(solution)/shard_map/write/pallas_call | solution.py:429

commit v7 on v6

--- a/solution.py
+++ b/solution.py
@@ -13,7 +13,8 @@
 GROUP = 8
 CHUNKS = 8
 PIECES = 8
-PARTS = (32, 16, 8, 8)
+LOADS = 2
+PARTS = (40, 16, 8)
 HALO = 3
 ORDER1 = (6, 0, 4, 2, 7, 1, 5, 3)
 ORDER3 = (1, 0, 7, 6, 2, 3, 4, 5)
@@ -132,10 +133,10 @@
             signal(barrier, gx=me + 1 - lax.rem(p, 2), gz=other)
 
     def load(n):
-        part = pl.ds(n * wide, wide)
+        part = pl.ds(n * (cells // LOADS), cells // LOADS)
         return pltpu.make_async_copy(v_hbm.at[:, part], v_ref.at[:, part], load_sem.at[n])
 
-    for n in range(CHUNKS):
+    for n in range(LOADS):
         load(n).start()
 
     def halo(n, side):
@@ -174,7 +175,6 @@
         return fields_of([F32(scale) * a for a in v], v)
 
     def forward(n, state):
-        load(n).wait()
         ahead, back, weight = state
         for u in range(wide):
             x = n * wide + u
@@ -193,7 +193,10 @@
     pl.when(jnp.logical_and(even, p >= GROUP // 2))(pass_on)
 
     state = ((zero,) * 9, (zero,) * 9, jnp.ones(shape, F32))
-    state = lax.fori_loop(0, CHUNKS, forward, state)
+    each = CHUNKS // LOADS
+    for n in range(LOADS):
+        load(n).wait()
+        state = lax.fori_loop(n * each, (n + 1) * each, forward, state)
     for i in range(9):
         sums_ref[i] = state[0][i]
         sums_ref[9 + i] = state[1][i]
@@ -412,7 +415,7 @@
         ]
         + [pltpu.VMEM(small, F32)] * 6
         + [
-            pltpu.SemaphoreType.DMA((CHUNKS,)),
+            pltpu.SemaphoreType.DMA((LOADS,)),
             pltpu.SemaphoreType.DMA,
             pltpu.SemaphoreType.DMA((len(PARTS),)),
             pltpu.SemaphoreType.DMA((3,)),

time: 26 us -> 26 us (level)
  no operation moved by 1% of the time
where the time goes in v7:
time: 26 us; the launch traced here: 25.9 us
  Pallas kernels  25.2 us (97%)
  between operations  0.64 us (2%)
    pallas_call x1, Pallas kernels, shards(): pl.pallas_call(functools.partial(exchange_kernel, decay, scale, cells, bl...  21.6 us
    pallas_call x1, Pallas kernels, shards(): pl.pallas_call(functools.partial(write_kernel, decay, cells), out_shape=(...  3.63 us

profile of v7, /device:TPU:1, one launch (start us, length us, event | category | flops | bytes accessed | tf_op | source)
XLA Modules:
  0.0 25.9 jit_solution(12335541906183004616)
XLA Ops:
  0.6 21.6 %exchange.1 = (f32[9,64,8,256]{3,2,1,0:T(8,128)S(1)}, f32[9,64,8,256]{3,2,1,0:T(8,128)S(1)}, f32[18,8,256]{2,1,0:T(8,128)S(1)}) custom-call(f32[3,64,8,256]{3,2,1,0:T(8,128)} %v_hbm.1), custom_call_target="tpu_custom_call" | custom-call | tf_op jit(solution)/shard_map/exchange/pallas_call | solution.py:403
  22.2 3.6 %write.1 = (f32[9,64,8,256]{3,2,1,0:T(8,128)}, f32[9,64,8,256]{3,2,1,0:T(8,128)}) custom-call(f32[9,64,8,256]{3,2,1,0:T(8,128)S(1)} %get-tuple-element.5.local_ref, f32[9,64,8,256]{3,2,1,0:T(8,128)S(1)} %get-tuple-element.6.deriv_ref, f32[18,8,256]{2,1,0:T(8,128)S(1)} %get-tuple-element.7.carry_ref), custom_call_target="tpu_custom_call" | custom-call | tf_op jit(solution)/shard_map/write/pallas_call | solution.py:432
